TPU v7x, 32 devices: a whole 2x2x4 slice. The times are simulated.
32 devices in a mesh: section: 2 (over y), dp: 4 (over z), tensor: 4 (over x, core).
Axes of the slice: x: 2, y: 2, z: 4, core: 2. Of those that a mesh axis runs over, the one named last changes fastest.
Arguments:
- layer_input: bfloat16 [2, 2, 256, 8192], P('section', None, 'tensor', 'dp'), may hold values from -64 to 64
- ready_grad: bfloat16 [2, 256, 8192], P('section', 'tensor', 'dp'), may hold values from -6 to 6
- late_grad: bfloat16 [256, 8192], P('tensor', 'dp'), may hold values from -6 to 6
- norm_gain: float32 [2, 8192], P('section', 'dp'), may hold values from 0.25 to 4.5
- norm_bias: float32 [2, 8192], P('section', 'dp'), may hold values from -3 to 3
- up_weight: bfloat16 [2, 8192, 16384], P('section', 'dp', 'tensor'), may hold values from -0.0625 to 0.0625
- down_weight: bfloat16 [2, 16384, 8192], P('section', 'tensor', 'dp'), may hold values from -0.046875 to 0.046875
Outputs:
- input_grad: bfloat16 [2, 2, 256, 8192], P('section', None, 'tensor', 'dp')
- up_grad: bfloat16 [2, 8192, 16384], P('section', 'dp', 'tensor')
- down_grad: bfloat16 [2, 16384, 8192], P('section', 'tensor', 'dp')
- gain_grad: float32 [2, 8192], P('section', 'dp')
- bias_grad: float32 [2, 8192], P('section', 'dp')
All inputs are finite; a program needn't handle non-finite values.
Results may differ from a plain program's by a relative error of at most 0.03.
Values may be sent and summed in bfloat16 or wider, within the bound.
A program may use at most 192 MiB of HBM per device.

v0:
```python
import math
import jax
import jax.numpy as jnp
from jax import lax
from jax.sharding import PartitionSpec as P

MODEL_WIDTH = 8192
epsilon = 1e-05
inv_root_two = 0.7071067811865476
inv_root_two_pi = 0.3989422804014327


def from_behind(block, axis, distance):
    devices = range(lax.axis_size(axis))
    route = [(i - distance, i) for i in devices if i - distance in devices]
    return lax.ppermute(block, axis, route)


def gelu_value(values):
    return 0.5 * values * (1.0 + lax.erf(values * inv_root_two))


def gelu_slope(values):
    return (
        0.5 * (1.0 + lax.erf(values * inv_root_two))
        + values * jnp.exp(-0.5 * values * values) * inv_root_two_pi
    )


def round_partial(partial_value):
    return lax.optimization_barrier(partial_value.astype(jnp.bfloat16)).astype(jnp.float32)


def section_pass(inputs_tile, incoming_gradient, scale_gain, shift_bias, weight_up, weight_down):
    tensor_rows = inputs_tile.shape[0]
    inputs_float = inputs_tile.astype(jnp.float32)
    row_total, row_squares = lax.psum(
        (
            jnp.sum(inputs_float, axis=1, keepdims=True),
            jnp.sum(inputs_float * inputs_float, axis=1, keepdims=True),
        ),
        "dp",
    )
    row_mean = row_total / MODEL_WIDTH
    variance = row_squares / MODEL_WIDTH - row_mean * row_mean
    inverse_deviation = lax.rsqrt(variance + epsilon)
    centered_input = (inputs_float - row_mean) * inverse_deviation
    normalized = (centered_input * scale_gain + shift_bias).astype(jnp.bfloat16)
    normed_all = lax.all_gather(normalized, "tensor", axis=0, tiled=True)
    left_rows = normed_all
    pre_rows = lax.psum_scatter(
        round_partial(jnp.dot(left_rows, weight_up, preferred_element_type=jnp.float32)).astype(
            jnp.bfloat16
        ),
        "dp",
        scatter_dimension=0,
        tiled=True,
    ).astype(jnp.float32)
    act_all = lax.all_gather(gelu_value(pre_rows).astype(jnp.bfloat16), "dp", axis=0, tiled=True)
    slope = gelu_slope(pre_rows)
    down_term = jnp.dot(act_all.T, incoming_gradient, preferred_element_type=jnp.float32)
    left_rows = incoming_gradient
    act_grad = lax.psum_scatter(
        round_partial(
            lax.dot_general(
                left_rows, weight_down, (((1,), (1,)), ((), ())), preferred_element_type=jnp.float32
            )
        ).astype(jnp.bfloat16),
        "dp",
        scatter_dimension=0,
        tiled=True,
    ).astype(jnp.float32)
    pre_grad = (act_grad * slope).astype(jnp.bfloat16)
    pre_grad_all = lax.all_gather(pre_grad, "dp", axis=0, tiled=True)
    up_term = jnp.dot(normed_all.T, pre_grad_all, preferred_element_type=jnp.float32)
    left_rows = pre_grad_all
    normalized_gradient = lax.psum_scatter(
        lax.dot_general(
            left_rows, weight_up, (((1,), (1,)), ((), ())), preferred_element_type=jnp.float32
        ).astype(jnp.bfloat16),
        "tensor",
        scatter_dimension=0,
        tiled=True,
    ).astype(jnp.float32)
    gain_product = jnp.sum(normalized_gradient * centered_input, axis=0)
    bias_term = jnp.sum(normalized_gradient, axis=0)
    centered_gradient = normalized_gradient * scale_gain
    centered_total, centered_cross = lax.psum(
        (
            jnp.sum(centered_gradient, axis=1, keepdims=True),
            jnp.sum(centered_gradient * centered_input, axis=1, keepdims=True),
        ),
        "dp",
    )
    local_rows = lax.dynamic_slice_in_dim(
        incoming_gradient, lax.axis_index("tensor") * tensor_rows, tensor_rows, 0
    ).astype(jnp.float32)
    final_output = local_rows + inverse_deviation * (
        centered_gradient
        - centered_total / MODEL_WIDTH
        - centered_input * (centered_cross / MODEL_WIDTH)
    )
    return (final_output.astype(jnp.bfloat16), down_term, up_term, gain_product, bias_term)


def body(layer_input, ready_grad, late_grad, norm_gain, norm_bias, up_weight, down_weight):
    early = lax.axis_index("section") == 0
    scale_gain = norm_gain[0]
    shift_bias = norm_bias[0]
    weight_up = up_weight[0]
    weight_down = down_weight[0]
    ready_whole, late_whole = (
        lax.all_gather(ready_grad[0], "tensor", axis=0, tiled=True),
        lax.all_gather(late_grad, "tensor", axis=0, tiled=True),
    )
    first_pass = section_pass(
        layer_input[0, 0], ready_whole, scale_gain, shift_bias, weight_up, weight_down
    )
    sent = first_pass[0]
    assembled = lax.all_gather(sent, "tensor", axis=0, tiled=True)
    arrived = from_behind(assembled, "section", -1)
    second_incoming = jnp.where(early, arrived, late_whole)
    second_pass = section_pass(
        layer_input[0, 1], second_incoming, scale_gain, shift_bias, weight_up, weight_down
    )
    scale = 1.0 / math.sqrt(2 * second_incoming.shape[0])
    down_part = ((first_pass[1] + second_pass[1]) * scale).astype(jnp.bfloat16)
    up_part = ((first_pass[2] + second_pass[2]) * scale).astype(jnp.bfloat16)
    gain_sum, bias_sum = lax.psum(
        (first_pass[3] + second_pass[3], first_pass[4] + second_pass[4]), "tensor"
    )
    results = jnp.stack([first_pass[0], second_pass[0]])
    return (
        results[None],
        up_part[None],
        down_part[None],
        (gain_sum * scale)[None],
        (bias_sum * scale)[None],
    )


def solution(mesh):
    in_specs = (
        P("section", None, "tensor", "dp"),
        P("section", "tensor", "dp"),
        P("tensor", "dp"),
        P("section", "dp"),
        P("section", "dp"),
        P("section", "dp", "tensor"),
        P("section", "tensor", "dp"),
    )
    out_specs = (
        P("section", None, "tensor", "dp"),
        P("section", "dp", "tensor"),
        P("section", "tensor", "dp"),
        P("section", "dp"),
        P("section", "dp"),
    )
    return jax.shard_map(body, mesh=mesh, in_specs=in_specs, out_specs=out_specs, check_vma=False)
```

profile of v0, /device:TPU:0, one launch (start us, length us, event | category | flops | bytes accessed | tf_op | source)
XLA Modules:
  0.0 594.6 jit_solution(13825570276484820397)
XLA Ops:
  9.5 13.5 %all-reduce.3 = (f32[64,1]{0,1:T(1,128)S(1)}, f32[64,1]{0,1:T(1,128)S(1)}) all-reduce(f32[64,1]{0,1:T(1,128)S(1)} %bitcast.170, f32[64,1]{0,1:T(1,128)S(1)} %bitcast.167), channel_id=1, replica_groups=mesh['section'=2,'dp'=4,'tensor'=4] {'dp'}, use_global_device_ids=true, to_apply=%region_3.0 | all-reduce | flops 128 | bytes 1024 | tf_op jit(solution)/shard_map/psum | solution.py:37
  25.7 14.3 %all-gather.11.cloned.1.call-done = bf16[256,2048]{1,0:T(8,128)(2,1)} async-done(((bf16[64,2048]{1,0:T(8,128)(2,1)}), bf16[256,2048]{1,0:T(8,128)(2,1)}) %all-gather.11.cloned.1.call-update) | async-done | bytes 1048592 | tf_op jit(solution)/shard_map/all_gather | solution.py:49
  40.0 11.9 %fusion.20 = bf16[256,4096]{1,0:T(8,128)(2,1)} fusion(bf16[256,2048]{1,0:T(8,128)(2,1)} %all-gather.11.cloned.1.call-done, bf16[1,2048,4096]{2,1,0:T(8,128)(2,1)} %param.12), kind=kOutput, calls=%fused_computation.18 | convolution fusion | flops 4296015872 | bytes 19922944 | tf_op jit(solution)/shard_map/dot_general | solution.py:52
  52.0 6.3 %all-gather.27.cloned.1.call-done = bf16[1,256,2048]{2,1,0:T(8,128)(2,1)} async-done(((bf16[1,64,2048]{2,1,0:T(8,128)(2,1)}), bf16[1,256,2048]{2,1,0:T(8,128)(2,1)}) %all-gather.27.cloned.1.call-update) | async-done | bytes 1048592 | tf_op jit(solution)/shard_map/all_gather | solution.py:113
  58.3 12.0 %fusion.14 = bf16[256,4096]{1,0:T(8,128)(2,1)} fusion(bf16[1,4096,2048]{2,1,0:T(8,128)(2,1)} %param.13, bf16[1,256,2048]{2,1,0:T(8,128)(2,1)} %all-gather.27.cloned.1.call-done), kind=kOutput, calls=%fused_computation.16 | convolution fusion | flops 4296015872 | bytes 19922944 | tf_op jit(solution)/shard_map/dot_general | solution.py:65
  70.3 34.7 %reduce-scatter.9.cloned.1.call-done = bf16[64,4096]{1,0:T(8,128)(2,1)} async-done(((bf16[256,4096]{1,0:T(8,128)(2,1)}), bf16[64,4096]{1,0:T(8,128)(2,1)}) %reduce-scatter.9.cloned.1.call-update) | async-done | bytes 524304 | tf_op jit(solution)/shard_map/reduce_scatter | solution.py:51
  105.1 46.0 %reduce-scatter.7.cloned.1.call-done = bf16[64,4096]{1,0:T(8,128)(2,1)} async-done(((bf16[256,4096]{1,0:T(8,128)(2,1)}), bf16[64,4096]{1,0:T(8,128)(2,1)}) %reduce-scatter.7.cloned.1.call-update) | async-done | bytes 524304 | tf_op jit(solution)/shard_map/reduce_scatter | solution.py:63
  151.1 2.7 fusion.40
  154.4 44.9 %all-gather.13.cloned.1.call-done = bf16[256,4096]{1,0:T(8,128)(2,1)} async-done(((bf16[64,4096]{1,0:T(8,128)(2,1)}), bf16[256,4096]{1,0:T(8,128)(2,1)}) %all-gather.13.cloned.1.call-update) | async-done | bytes 2097168 | tf_op jit(solution)/shard_map/all_gather | solution.py:74
  199.3 11.9 %fusion.26 = bf16[256,2048]{1,0:T(8,128)(2,1)} fusion(bf16[256,4096]{1,0:T(8,128)(2,1)} %all-gather.13.cloned.1.call-done, bf16[1,2048,4096]{2,1,0:T(8,128)(2,1)} %param.12), kind=kOutput, calls=%fused_computation.20 | convolution fusion | flops 4295491584 | bytes 19922944 | tf_op jit(solution)/shard_map/dot_general | solution.py:78
  211.3 23.7 %reduce-scatter.11.cloned.1.call-done = bf16[64,2048]{1,0:T(8,128)(2,1)} async-done(((bf16[256,2048]{1,0:T(8,128)(2,1)}), bf16[64,2048]{1,0:T(8,128)(2,1)}) %reduce-scatter.11.cloned.1.call-update) | async-done | bytes 262160 | tf_op jit(solution)/shard_map/reduce_scatter | solution.py:77
  236.4 11.7 %all-reduce.2 = (f32[64,1]{0,1:T(1,128)S(1)}, f32[64,1]{0,1:T(1,128)S(1)}, f32[64,1]{0,1:T(1,128)S(1)}, f32[64,1]{0,1:T(1,128)S(1)}) all-reduce(f32[64,1]{0,1:T(1,128)S(1)} %bitcast.163, f32[64,1]{0,1:T(1,128)S(1)} %bitcast.165, f32[64,1]{0,1:T(1,128)S(1)} %bitcast.164, ...), channel_id=1, replica_groups=mesh['section'=2,'dp'=4,'tensor'=4] {'dp'}, use_global_device_ids=true, to_apply=%region_14.15 | all-reduce | flops 256 | bytes 2048 | tf_op jit(solution)/shard_map/psum | solution.py:37
  251.7 12.6 %all-gather.19.cloned.1.call-done = bf16[256,2048]{1,0:T(8,128)(2,1)} async-done(((bf16[64,2048]{1,0:T(8,128)(2,1)}), bf16[256,2048]{1,0:T(8,128)(2,1)}) %all-gather.19.cloned.1.call-update) | async-done | bytes 1048592 | tf_op jit(solution)/shard_map/all_gather | solution.py:49
  264.3 11.9 %fusion.23 = bf16[256,4096]{1,0:T(8,128)(2,1)} fusion(bf16[256,2048]{1,0:T(8,128)(2,1)} %all-gather.19.cloned.1.call-done, bf16[1,2048,4096]{2,1,0:T(8,128)(2,1)} %param.12), kind=kOutput, calls=%fused_computation.19 | convolution fusion | flops 4296015872 | bytes 19922944 | tf_op jit(solution)/shard_map/dot_general | solution.py:52
  276.3 6.4 %all-gather.15.cloned.1.call-done = bf16[256,2048]{1,0:T(8,128)(2,1)} async-done(((bf16[64,2048]{1,0:T(8,128)(2,1)}), bf16[256,2048]{1,0:T(8,128)(2,1)}) %all-gather.15.cloned.1.call-update) | async-done | bytes 1048592 | tf_op jit(solution)/shard_map/all_gather | solution.py:120
  284.2 16.9 %all-gather.17.cloned.1.call-done = bf16[256,2048]{1,0:T(8,128)(2,1)} async-done(((bf16[64,2048]{1,0:T(8,128)(2,1)}), bf16[256,2048]{1,0:T(8,128)(2,1)}) %all-gather.17.cloned.1.call-update) | async-done | bytes 1048592 | tf_op jit(solution)/shard_map/all_gather | solution.py:114
  301.1 9.1 %collective-permute-done = bf16[256,2048]{1,0:T(8,128)(2,1)} collective-permute-done((bf16[256,2048]{1,0:T(8,128)(2,1)}, bf16[256,2048]{1,0:T(8,128)(2,1)}, u32[]{:S(2)}, u32[]{:S(2)}) %collective-permute-start) | collective-permute-done | bytes 1048608 | tf_op jit(solution)/shard_map/ppermute | solution.py:16
  311.6 18.1 %fusion.17 = bf16[256,4096]{1,0:T(8,128)(2,1)} fusion(bf16[256,2048]{1,0:T(8,128)(2,1)S(1)} %broadcast_select_fusion, bf16[1,4096,2048]{2,1,0:T(8,128)(2,1)} %param.13), kind=kOutput, calls=%fused_computation.17 | convolution fusion | flops 4296015872 | bytes 19922944 | tf_op jit(solution)/shard_map/dot_general | solution.py:65
  330.3 17.5 %reduce-scatter.15.cloned.1.call-done = bf16[64,4096]{1,0:T(8,128)(2,1)} async-done(((bf16[256,4096]{1,0:T(8,128)(2,1)}), bf16[64,4096]{1,0:T(8,128)(2,1)}) %reduce-scatter.15.cloned.1.call-update) | async-done | bytes 524304 | tf_op jit(solution)/shard_map/reduce_scatter | solution.py:51
  347.8 46.1 %reduce-scatter.13.cloned.1.call-done = bf16[64,4096]{1,0:T(8,128)(2,1)} async-done(((bf16[256,4096]{1,0:T(8,128)(2,1)}), bf16[64,4096]{1,0:T(8,128)(2,1)}) %reduce-scatter.13.cloned.1.call-update) | async-done | bytes 524304 | tf_op jit(solution)/shard_map/reduce_scatter | solution.py:63
  393.9 2.7 fusion.49
  397.3 17.7 %fusion.88 = f32[2048,4096]{1,0:T(8,128)} fusion(bf16[256,2048]{1,0:T(8,128)(2,1)} %all-gather.11.cloned.1.call-done, bf16[256,4096]{1,0:T(8,128)(2,1)} %all-gather.13.cloned.1.call-done), kind=kOutput, calls=%fused_computation.110 | convolution fusion | flops 4294967296 | bytes 36700160 | tf_op jit(solution)/shard_map/dot_general | solution.py:75
  415.0 26.3 %all-gather.23.cloned.1.call-done = bf16[256,4096]{1,0:T(8,128)(2,1)} async-done(((bf16[64,4096]{1,0:T(8,128)(2,1)}), bf16[256,4096]{1,0:T(8,128)(2,1)}) %all-gather.23.cloned.1.call-update) | async-done | bytes 2097168 | tf_op jit(solution)/shard_map/all_gather | solution.py:59
  441.3 15.4 %fusion.51 = f32[4096,2048]{1,0:T(8,128)} fusion(bf16[256,4096]{1,0:T(8,128)(2,1)} %all-gather.23.cloned.1.call-done, bf16[1,256,2048]{2,1,0:T(8,128)(2,1)S(1)} %copy-done.2), kind=kOutput, calls=%fused_computation.51 | convolution fusion | flops 4294967296 | bytes 36700160 | tf_op jit(solution)/shard_map/dot_general | solution.py:61
  456.7 31.5 %all-gather.21.cloned.1.call-done = bf16[256,4096]{1,0:T(8,128)(2,1)} async-done(((bf16[64,4096]{1,0:T(8,128)(2,1)}), bf16[256,4096]{1,0:T(8,128)(2,1)}) %all-gather.21.cloned.1.call-update) | async-done | bytes 2097168 | tf_op jit(solution)/shard_map/all_gather | solution.py:74
  488.2 11.9 %fusion.29 = bf16[256,2048]{1,0:T(8,128)(2,1)} fusion(bf16[256,4096]{1,0:T(8,128)(2,1)} %all-gather.21.cloned.1.call-done, bf16[1,2048,4096]{2,1,0:T(8,128)(2,1)} %param.12), kind=kOutput, calls=%fused_computation.21 | convolution fusion | flops 4295491584 | bytes 19922944 | tf_op jit(solution)/shard_map/dot_general | solution.py:78
  500.2 17.7 %fusion = bf16[1,2048,4096]{2,1,0:T(8,128)(2,1)} fusion(f32[2048,4096]{1,0:T(8,128)} %fusion.88, bf16[256,2048]{1,0:T(8,128)(2,1)S(1)} %copy-done.3, bf16[256,4096]{1,0:T(8,128)(2,1)} %all-gather.21.cloned.1.call-done), kind=kOutput, calls=%fused_computation.2 | convolution fusion | flops 4320133120 | bytes 53477376 | tf_op jit(solution)/shard_map/dot_general | solution.py:75
  517.8 17.1 %all-gather.25.cloned.1.call-done = bf16[256,4096]{1,0:T(8,128)(2,1)} async-done(((bf16[64,4096]{1,0:T(8,128)(2,1)}), bf16[256,4096]{1,0:T(8,128)(2,1)}) %all-gather.25.cloned.1.call-update) | async-done | bytes 2097168 | tf_op jit(solution)/shard_map/all_gather | solution.py:59
  534.9 17.7 %fusion.1 = bf16[1,4096,2048]{2,1,0:T(8,128)(2,1)} fusion(f32[4096,2048]{1,0:T(8,128)} %fusion.51, bf16[256,4096]{1,0:T(8,128)(2,1)} %all-gather.25.cloned.1.call-done, bf16[256,2048]{1,0:T(8,128)(2,1)S(1)} %broadcast_select_fusion), kind=kOutput, calls=%fused_computation.3 | convolution fusion | flops 4320133120 | bytes 53477376 | tf_op jit(solution)/shard_map/dot_general | solution.py:61
  552.7 8.5 %reduce-scatter.17.cloned.1.call-done = bf16[64,2048]{1,0:T(8,128)(2,1)} async-done(((bf16[256,2048]{1,0:T(8,128)(2,1)}), bf16[64,2048]{1,0:T(8,128)(2,1)}) %reduce-scatter.17.cloned.1.call-update) | async-done | bytes 262160 | tf_op jit(solution)/shard_map/reduce_scatter | solution.py:77
  562.5 11.7 %all-reduce.1 = (f32[64,1]{0,1:T(1,128)S(1)}, f32[64,1]{0,1:T(1,128)S(1)}) all-reduce(f32[64,1]{0,1:T(1,128)S(1)} %bitcast.168, f32[64,1]{0,1:T(1,128)S(1)} %bitcast.169), channel_id=1, replica_groups=mesh['section'=2,'dp'=4,'tensor'=4] {'dp'}, use_global_device_ids=true, to_apply=%region_21.22 | all-reduce | flops 128 | bytes 1024 | tf_op jit(solution)/shard_map/psum | solution.py:88
  574.2 10.3 %all-reduce = (f32[2048]{0:T(1024)S(1)}, f32[2048]{0:T(1024)S(1)}) all-reduce(f32[2048]{0:T(1024)S(1)} %add.105, f32[2048]{0:T(1024)S(1)} %add.106), channel_id=1, replica_groups=mesh['section'=2,'dp'=4,'tensor'=4] {'tensor'}, use_global_device_ids=true, to_apply=%region_24.25 | all-reduce | flops 4096 | bytes 32768 | tf_op jit(solution)/shard_map/psum | solution.py:129
  (61 shorter events, 19.5 us)
Async XLA Ops:
  7.2 32.8 %all-gather.11.cloned.1.call-start = ((), (), s32[]{:S(2)}) async-start(), calls=%async_computation.7 | async-start | bytes 1310720 | tf_op jit(solution)/shard_map/all_gather | solution.py:49
  24.9 33.4 %all-gather.27.cloned.1.call-start = ((), (), s32[]{:S(2)}) async-start(), calls=%async_computation.20 | async-start | bytes 1310720 | tf_op jit(solution)/shard_map/all_gather | solution.py:113
  25.6 79.4 %reduce-scatter.9.cloned.1.call-start = ((), (), s32[]{:S(2)}) async-start(), calls=%async_computation.8 | async-start | bytes 2621440 | tf_op jit(solution)/shard_map/reduce_scatter | solution.py:51
  51.9 99.2 %reduce-scatter.7.cloned.1.call-start = ((), (), s32[]{:S(2)}) async-start(), calls=%async_computation.6 | async-start | bytes 2621440 | tf_op jit(solution)/shard_map/reduce_scatter | solution.py:63
  70.3 164.7 %copy-start = (bf16[1,2,64,2048]{3,2,1,0:T(8,128)(2,1)S(1)}, bf16[1,2,64,2048]{3,2,1,0:T(8,128)(2,1)}, u32[]{:S(2)}) copy-start(bf16[1,2,64,2048]{3,2,1,0:T(8,128)(2,1)} %param.7) | copy-start | bytes 1572868
  70.3 164.7 %copy-start.4 = (f32[1,2048]{1,0:T(1,128)S(1)}, f32[1,2048]{1,0:T(1,128)}, u32[]{:S(2)}) copy-start(f32[1,2048]{1,0:T(1,128)} %param.10) | copy-start | bytes 24580
  70.3 129.0 %all-gather.13.cloned.1.call-start = ((), (), s32[]{:S(2)}) async-start(), calls=%async_computation.9 | async-start | bytes 2621440 | tf_op jit(solution)/shard_map/all_gather | solution.py:74
  153.8 94.2 %copy-start.2 = (bf16[1,256,2048]{2,1,0:T(8,128)(2,1)S(1)}, bf16[1,256,2048]{2,1,0:T(8,128)(2,1)}, u32[]{:S(2)}) copy-start(bf16[1,256,2048]{2,1,0:T(8,128)(2,1)} %all-gather.27.cloned.1.call-done) | copy-start | bytes 3145732
  153.9 94.2 %copy-start.5 = (f32[1,2048]{1,0:T(1,128)S(1)}, f32[1,2048]{1,0:T(1,128)}, u32[]{:S(2)}) copy-start(f32[1,2048]{1,0:T(1,128)} %param.11) | copy-start | bytes 24580
  153.9 81.1 %reduce-scatter.11.cloned.1.call-start = ((), (), s32[]{:S(2)}) async-start(), calls=%async_computation.10 | async-start | bytes 1310720 | tf_op jit(solution)/shard_map/reduce_scatter | solution.py:77
  211.2 53.1 %all-gather.19.cloned.1.call-start = ((), (), s32[]{:S(2)}) async-start(), calls=%async_computation.14 | async-start | bytes 1310720 | tf_op jit(solution)/shard_map/all_gather | solution.py:49
  250.2 32.5 %all-gather.15.cloned.1.call-start = ((), (), s32[]{:S(2)}) async-start(), calls=%async_computation.11 | async-start | bytes 1310720 | tf_op jit(solution)/shard_map/all_gather | solution.py:120
  250.9 50.2 %all-gather.17.cloned.1.call-start = ((), (), s32[]{:S(2)}) async-start(), calls=%async_computation.12 | async-start | bytes 1310720 | tf_op jit(solution)/shard_map/all_gather | solution.py:114
  251.7 96.2 %reduce-scatter.15.cloned.1.call-start = ((), (), s32[]{:S(2)}) async-start(), calls=%async_computation.15 | async-start | bytes 2621440 | tf_op jit(solution)/shard_map/reduce_scatter | solution.py:51
  276.3 117.7 %reduce-scatter.13.cloned.1.call-start = ((), (), s32[]{:S(2)}) async-start(), calls=%async_computation.13 | async-start | bytes 2621440 | tf_op jit(solution)/shard_map/reduce_scatter | solution.py:63
  282.7 27.5 %collective-permute-start = (bf16[256,2048]{1,0:T(8,128)(2,1)}, bf16[256,2048]{1,0:T(8,128)(2,1)}, u32[]{:S(2)}, u32[]{:S(2)}) collective-permute-start(bf16[256,2048]{1,0:T(8,128)(2,1)} %all-gather.15.cloned.1.call-done), channel_id=1, source_target_pairs={{16,0},{17,1},{18,2},{19,3},{20,4},{21,5},{22,6},{23,7},{24,8},{25... | collective-permute-start | bytes 3145736 | tf_op jit(solution)/shard_map/ppermute | solution.py:16
  329.7 111.6 %all-gather.23.cloned.1.call-start = ((), (), s32[]{:S(2)}) async-start(), calls=%async_computation.18 | async-start | bytes 2621440 | tf_op jit(solution)/shard_map/all_gather | solution.py:59
  330.2 158.0 %all-gather.21.cloned.1.call-start = ((), (), s32[]{:S(2)}) async-start(), calls=%async_computation.16 | async-start | bytes 2621440 | tf_op jit(solution)/shard_map/all_gather | solution.py:74
  396.7 138.3 %all-gather.25.cloned.1.call-start = ((), (), s32[]{:S(2)}) async-start(), calls=%async_computation.19 | async-start | bytes 2621440 | tf_op jit(solution)/shard_map/all_gather | solution.py:59
  397.3 163.9 %reduce-scatter.17.cloned.1.call-start = ((), (), s32[]{:S(2)}) async-start(), calls=%async_computation.17 | async-start | bytes 1310720 | tf_op jit(solution)/shard_map/reduce_scatter | solution.py:77
  456.7 43.5 %copy-start.3 = (bf16[256,2048]{1,0:T(8,128)(2,1)S(1)}, bf16[256,2048]{1,0:T(8,128)(2,1)}, u32[]{:S(2)}) copy-start(bf16[256,2048]{1,0:T(8,128)(2,1)} %all-gather.19.cloned.1.call-done) | copy-start | bytes 3145732
  517.8 69.2 %copy-start.1 = (bf16[64,2048]{1,0:T(8,128)(2,1)S(1)}, bf16[64,2048]{1,0:T(8,128)(2,1)}, u32[]{:S(2)}) copy-start(bf16[64,2048]{1,0:T(8,128)(2,1)} %get-tuple-element.26) | copy-start | bytes 786436
Sparse Core Ops, SparseCore 0:
  25.0 14.9 all-gather.10
  41.5 16.7 all-gather.26
  61.2 43.8 reduce-scatter.8
  107.9 43.1 reduce-scatter.6
  154.0 45.2 all-gather.12
  211.3 23.5 reduce-scatter.10
  250.3 13.9 all-gather.18
  265.9 16.7 all-gather.14
  284.3 16.7 all-gather.16
  303.9 43.8 reduce-scatter.14
  350.7 43.1 reduce-scatter.12
  396.0 45.2 all-gather.22
  443.5 44.6 all-gather.20
  490.3 44.6 all-gather.24
  537.5 23.6 reduce-scatter.16
where the time goes:
time: 602 us; the launch traced here: 595 us
  waiting for transfers between devices  365 us (61%)
  matrix products  146 us (24%)
  blocking collectives  47.1 us (8%)
  other arithmetic  19.2 us (3%)
  between operations  14.3 us (2%)
    reduce_scatter x2, waiting for transfers between devices, section_pass(): lax.psum_scatter(round_partial(lax.dot_general(left_rows, weight_down, ((...  92.1 us
    all_gather x2, waiting for transfers between devices, section_pass(): pre_grad_all = lax.all_gather(pre_grad, 'dp', axis=0, tiled=True)  76.4 us
    reduce_scatter x2, waiting for transfers between devices, section_pass(): lax.psum_scatter(round_partial(jnp.dot(left_rows, weight_up, preferred_el...  52.3 us
    all_gather x2, waiting for transfers between devices, section_pass(): lax.all_gather(gelu_value(pre_rows).astype(jnp.bfloat16), 'dp', axis=0, t...  43.4 us
    dot_general x2, matrix products, section_pass(): jnp.dot(normed_all.T, pre_grad_all, preferred_element_type=jnp.float32)  35.3 us
    dot_general x2, matrix products, section_pass(): jnp.dot(act_all.T, incoming_gradient, preferred_element_type=jnp.float32)  33.1 us
    reduce_scatter x2, waiting for transfers between devices, section_pass(): lax.psum_scatter(lax.dot_general(left_rows, weight_up, (((1,), (1,)), (()...  32.2 us
    dot_general x2, matrix products, section_pass(): lax.dot_general(left_rows, weight_down, (((1,), (1,)), ((), ())), preferr...  30 us
  transfers between devices with their start and end apart: 16, of which 16 were waited for; matrix products, arithmetic and copies ran while one was open for 23% of the time, Pallas kernels for 0%

commit v1 on v0

--- a/solution.py
+++ b/solution.py
@@ -56,7 +56,17 @@
         scatter_dimension=0,
         tiled=True,
     ).astype(jnp.float32)
-    act_all = lax.all_gather(gelu_value(pre_rows).astype(jnp.bfloat16), "dp", axis=0, tiled=True)
+    x = gelu_value(pre_rows).astype(jnp.bfloat16)
+    ways = lax.axis_size("dp")
+    up = [(d, (d + 1) % ways) for d in range(ways)]
+    down = [(d, (d - 1) % ways) for d in range(ways)]
+    earlier, later = ([x], [x])
+    for _ in range(ways // 2):
+        earlier.append(lax.ppermute(earlier[-1], "dp", up))
+    for _ in range((ways - 1) // 2):
+        later.append(lax.ppermute(later[-1], "dp", down))
+    line = jnp.concatenate([*earlier[::-1], *later[1:]], axis=0)
+    act_all = jnp.roll(line, (lax.axis_index("dp") - ways // 2) * x.shape[0], axis=0)
     slope = gelu_slope(pre_rows)
     down_term = jnp.dot(act_all.T, incoming_gradient, preferred_element_type=jnp.float32)
     left_rows = incoming_gradient

time: 602 us -> 609 us (1.012)
  starting transfers between devices: 2.52 us -> 20.5 us
  waiting for transfers between devices: 365 us -> 352 us
  matrix products: 146 us -> 153 us
    ppermute x0 -> x6, waiting for transfers between devices: none -> 59.8 us  [the longest x2 35.9 us: section_pass(): later.append(lax.ppermute(later[-1], 'dp', down))]
    all_gather x2 -> x0, waiting for transfers between devices: 43.4 us -> none  [section_pass(): lax.all_gather(gelu_value(pre_rows).astype(jnp.bfloat16), 'dp', axis=0, t...]
    all_gather x2, waiting for transfers between devices: 76.4 us -> 44.8 us  [section_pass(): pre_grad_all = lax.all_gather(pre_grad, 'dp', axis=0, tiled=True)]
    ppermute x0 -> x6, starting transfers between devices: none -> 18 us  [the longest x4 10.3 us: section_pass(): earlier.append(lax.ppermute(earlier[-1], 'dp', up))]
    reduce_scatter x2, waiting for transfers between devices: 52.3 us -> 63.8 us  [section_pass(): lax.psum_scatter(round_partial(jnp.dot(left_rows, weight_up, preferred_el...]
    reduce_scatter x2, waiting for transfers between devices: 32.2 us -> 23.7 us  [section_pass(): lax.psum_scatter(lax.dot_general(left_rows, weight_up, (((1,), (1,)), (()...]
  transfers between devices with their start and end apart: 16 -> 20, of which waited for: 16 -> 15; matrix products, arithmetic and copies ran while one was open for 23% -> 24% of each run, Pallas kernels for 0% -> 0%
where the time goes in v1:
time: 609 us; the launch traced here: 601 us
  waiting for transfers between devices  352 us (58%)
  matrix products  153 us (25%)
  blocking collectives  43.7 us (7%)
  starting transfers between devices  20.5 us (3%)
  other arithmetic  17.7 us (3%)
  between operations  14.3 us (2%)
    reduce_scatter x2, waiting for transfers between devices, section_pass(): lax.psum_scatter(round_partial(lax.dot_general(left_rows, weight_down, ((...  92.2 us
    reduce_scatter x2, waiting for transfers between devices, section_pass(): lax.psum_scatter(round_partial(jnp.dot(left_rows, weight_up, preferred_el...  63.8 us
    all_gather x2, waiting for transfers between devices, section_pass(): pre_grad_all = lax.all_gather(pre_grad, 'dp', axis=0, tiled=True)  44.8 us
    dot_general x2, matrix products, section_pass(): jnp.dot(act_all.T, incoming_gradient, preferred_element_type=jnp.float32)  38.3 us
    dot_general x2, matrix products, section_pass(): jnp.dot(normed_all.T, pre_grad_all, preferred_element_type=jnp.float32)  37.3 us
    ppermute x2, waiting for transfers between devices, section_pass(): later.append(lax.ppermute(later[-1], 'dp', down))  35.9 us
    dot_general x2, matrix products, section_pass(): lax.dot_general(left_rows, weight_down, (((1,), (1,)), ((), ())), preferr...  30 us
    all_gather x2, waiting for transfers between devices, section_pass(): normed_all = lax.all_gather(normalized, 'tensor', axis=0, tiled=True)  26.9 us
  transfers between devices with their start and end apart: 20, of which 15 were waited for; matrix products, arithmetic and copies ran while one was open for 24% of the time, Pallas kernels for 0%

profile of v1, /device:TPU:0, one launch (start us, length us, event | category | flops | bytes accessed | tf_op | source)
XLA Modules:
  0.0 601.5 jit_solution(10761048125505678709)
XLA Ops:
  9.5 13.5 %all-reduce.3 = (f32[64,1]{0,1:T(1,128)S(1)}, f32[64,1]{0,1:T(1,128)S(1)}) all-reduce(f32[64,1]{0,1:T(1,128)S(1)} %bitcast.168, f32[64,1]{0,1:T(1,128)S(1)} %bitcast.165), channel_id=1, replica_groups=mesh['section'=2,'dp'=4,'tensor'=4] {'dp'}, use_global_device_ids=true, to_apply=%region_3.0 | all-reduce | flops 128 | bytes 1024 | tf_op jit(solution)/shard_map/psum | solution.py:37
  25.7 14.3 %all-gather.9.cloned.1.call-done = bf16[256,2048]{1,0:T(8,128)(2,1)} async-done(((bf16[64,2048]{1,0:T(8,128)(2,1)}), bf16[256,2048]{1,0:T(8,128)(2,1)}) %all-gather.9.cloned.1.call-update) | async-done | bytes 1048592 | tf_op jit(solution)/shard_map/all_gather | solution.py:49
  40.0 11.9 %fusion.20 = bf16[256,4096]{1,0:T(8,128)(2,1)} fusion(bf16[256,2048]{1,0:T(8,128)(2,1)} %all-gather.9.cloned.1.call-done, bf16[1,2048,4096]{2,1,0:T(8,128)(2,1)} %param.14), kind=kOutput, calls=%fused_computation.18 | convolution fusion | flops 4296015872 | bytes 19922944 | tf_op jit(solution)/shard_map/dot_general | solution.py:52
  52.0 6.3 %all-gather.21.cloned.1.call-done = bf16[1,256,2048]{2,1,0:T(8,128)(2,1)} async-done(((bf16[1,64,2048]{2,1,0:T(8,128)(2,1)}), bf16[1,256,2048]{2,1,0:T(8,128)(2,1)}) %all-gather.21.cloned.1.call-update) | async-done | bytes 1048592 | tf_op jit(solution)/shard_map/all_gather | solution.py:123
  58.3 12.0 %fusion.14 = bf16[256,4096]{1,0:T(8,128)(2,1)} fusion(bf16[1,4096,2048]{2,1,0:T(8,128)(2,1)} %param.15, bf16[1,256,2048]{2,1,0:T(8,128)(2,1)} %all-gather.21.cloned.1.call-done), kind=kOutput, calls=%fused_computation.16 | convolution fusion | flops 4296015872 | bytes 19922944 | tf_op jit(solution)/shard_map/dot_general | solution.py:75
  70.3 34.8 %reduce-scatter.9.cloned.1.call-done = bf16[64,4096]{1,0:T(8,128)(2,1)} async-done(((bf16[256,4096]{1,0:T(8,128)(2,1)}), bf16[64,4096]{1,0:T(8,128)(2,1)}) %reduce-scatter.9.cloned.1.call-update) | async-done | bytes 524304 | tf_op jit(solution)/shard_map/reduce_scatter | solution.py:51
  105.1 46.1 %reduce-scatter.7.cloned.1.call-done = bf16[64,4096]{1,0:T(8,128)(2,1)} async-done(((bf16[256,4096]{1,0:T(8,128)(2,1)}), bf16[64,4096]{1,0:T(8,128)(2,1)}) %reduce-scatter.7.cloned.1.call-update) | async-done | bytes 524304 | tf_op jit(solution)/shard_map/reduce_scatter | solution.py:73
  154.3 44.8 %all-gather.11.cloned.1.call-done = bf16[256,4096]{1,0:T(8,128)(2,1)} async-done(((bf16[64,4096]{1,0:T(8,128)(2,1)}), bf16[256,4096]{1,0:T(8,128)(2,1)}) %all-gather.11.cloned.1.call-update) | async-done | bytes 2097168 | tf_op jit(solution)/shard_map/all_gather | solution.py:84
  199.2 11.9 %fusion.26 = bf16[256,2048]{1,0:T(8,128)(2,1)} fusion(bf16[256,4096]{1,0:T(8,128)(2,1)} %all-gather.11.cloned.1.call-done, bf16[1,2048,4096]{2,1,0:T(8,128)(2,1)} %param.14), kind=kOutput, calls=%fused_computation.36 | convolution fusion | flops 4295491584 | bytes 19922944 | tf_op jit(solution)/shard_map/dot_general | solution.py:88
  211.1 23.7 %reduce-scatter.11.cloned.1.call-done = bf16[64,2048]{1,0:T(8,128)(2,1)} async-done(((bf16[256,2048]{1,0:T(8,128)(2,1)}), bf16[64,2048]{1,0:T(8,128)(2,1)}) %reduce-scatter.11.cloned.1.call-update) | async-done | bytes 262160 | tf_op jit(solution)/shard_map/reduce_scatter | solution.py:87
  236.2 11.7 %all-reduce.2 = (f32[64,1]{0,1:T(1,128)S(1)}, f32[64,1]{0,1:T(1,128)S(1)}, f32[64,1]{0,1:T(1,128)S(1)}, f32[64,1]{0,1:T(1,128)S(1)}) all-reduce(f32[64,1]{0,1:T(1,128)S(1)} %bitcast.161, f32[64,1]{0,1:T(1,128)S(1)} %bitcast.163, f32[64,1]{0,1:T(1,128)S(1)} %bitcast.162, ...), channel_id=1, replica_groups=mesh['section'=2,'dp'=4,'tensor'=4] {'dp'}, use_global_device_ids=true, to_apply=%region_14.15 | all-reduce | flops 256 | bytes 2048 | tf_op jit(solution)/shard_map/psum | solution.py:37
  251.6 12.6 %all-gather.17.cloned.1.call-done = bf16[256,2048]{1,0:T(8,128)(2,1)} async-done(((bf16[64,2048]{1,0:T(8,128)(2,1)}), bf16[256,2048]{1,0:T(8,128)(2,1)}) %all-gather.17.cloned.1.call-update) | async-done | bytes 1048592 | tf_op jit(solution)/shard_map/all_gather | solution.py:49
  264.2 11.9 %fusion.23 = bf16[256,4096]{1,0:T(8,128)(2,1)} fusion(bf16[256,2048]{1,0:T(8,128)(2,1)} %all-gather.17.cloned.1.call-done, bf16[1,2048,4096]{2,1,0:T(8,128)(2,1)} %param.14), kind=kOutput, calls=%fused_computation.19 | convolution fusion | flops 4296015872 | bytes 19922944 | tf_op jit(solution)/shard_map/dot_general | solution.py:52
  276.2 6.4 %all-gather.13.cloned.1.call-done = bf16[256,2048]{1,0:T(8,128)(2,1)} async-done(((bf16[64,2048]{1,0:T(8,128)(2,1)}), bf16[256,2048]{1,0:T(8,128)(2,1)}) %all-gather.13.cloned.1.call-update) | async-done | bytes 1048592 | tf_op jit(solution)/shard_map/all_gather | solution.py:130
  284.1 16.9 %all-gather.15.cloned.1.call-done = bf16[256,2048]{1,0:T(8,128)(2,1)} async-done(((bf16[64,2048]{1,0:T(8,128)(2,1)}), bf16[256,2048]{1,0:T(8,128)(2,1)}) %all-gather.15.cloned.1.call-update) | async-done | bytes 1048592 | tf_op jit(solution)/shard_map/all_gather | solution.py:124
  301.0 9.0 %collective-permute-done = bf16[256,2048]{1,0:T(8,128)(2,1)S(1)} collective-permute-done((bf16[256,2048]{1,0:T(8,128)(2,1)}, bf16[256,2048]{1,0:T(8,128)(2,1)S(1)}, u32[]{:S(2)}, u32[]{:S(2)}) %collective-permute-start) | collective-permute-done | bytes 1048608 | tf_op jit(solution)/shard_map/ppermute | solution.py:16
  310.1 18.1 %fusion.17 = bf16[256,4096]{1,0:T(8,128)(2,1)} fusion(bf16[256,2048]{1,0:T(8,128)(2,1)S(1)} %broadcast_select_fusion, bf16[1,4096,2048]{2,1,0:T(8,128)(2,1)} %param.15), kind=kOutput, calls=%fused_computation.17 | convolution fusion | flops 4296015872 | bytes 19922944 | tf_op jit(solution)/shard_map/dot_general | solution.py:75
  329.8 29.0 %reduce-scatter.15.cloned.1.call-done = bf16[64,4096]{1,0:T(8,128)(2,1)} async-done(((bf16[256,4096]{1,0:T(8,128)(2,1)}), bf16[64,4096]{1,0:T(8,128)(2,1)}) %reduce-scatter.15.cloned.1.call-update) | async-done | bytes 524304 | tf_op jit(solution)/shard_map/reduce_scatter | solution.py:51
  358.8 46.1 %reduce-scatter.13.cloned.1.call-done = bf16[64,4096]{1,0:T(8,128)(2,1)} async-done(((bf16[256,4096]{1,0:T(8,128)(2,1)}), bf16[64,4096]{1,0:T(8,128)(2,1)}) %reduce-scatter.13.cloned.1.call-update) | async-done | bytes 524304 | tf_op jit(solution)/shard_map/reduce_scatter | solution.py:73
  407.6 3.9 collective-permute-start.3
  411.5 3.8 collective-permute-start.6
  415.3 11.6 %collective-permute-done.4 = bf16[64,4096]{1,0:T(8,128)(2,1)S(1)} collective-permute-done((bf16[64,4096]{1,0:T(8,128)(2,1)S(1)}, bf16[64,4096]{1,0:T(8,128)(2,1)S(1)}, u32[]{:S(2)}, u32[]{:S(2)}) %collective-permute-start.4) | collective-permute-done | bytes 524320 | tf_op jit(solution)/shard_map/ppermute | solution.py:65
  426.9 8.7 %collective-permute-start.5 = (bf16[64,4096]{1,0:T(8,128)(2,1)S(1)}, bf16[64,4096]{1,0:T(8,128)(2,1)S(1)}, u32[]{:S(2)}, u32[]{:S(2)}) collective-permute-start(bf16[64,4096]{1,0:T(8,128)(2,1)S(1)} %collective-permute-done.4), channel_id=1, source_target_pairs={{0,4},{4,8},{8,12},{12,0},{1,5},{5,9},{9,13},{13,1},{2,6},{6,10},{... | collective-permute-start | bytes 1572872 | tf_op jit(solution)/shard_map/ppermute | solution.py:65
  435.7 17.7 %fusion.110 = f32[2048,4096]{1,0:T(8,128)} fusion(bf16[256,2048]{1,0:T(8,128)(2,1)} %all-gather.9.cloned.1.call-done, bf16[256,4096]{1,0:T(8,128)(2,1)} %all-gather.11.cloned.1.call-done), kind=kOutput, calls=%fused_computation.144 | convolution fusion | flops 4294967296 | bytes 36700160 | tf_op jit(solution)/shard_map/dot_general | solution.py:85
  453.4 35.9 %collective-permute-done.6 = bf16[64,4096]{1,0:T(8,128)(2,1)S(1)} collective-permute-done((bf16[64,4096]{1,0:T(8,128)(2,1)S(1)}, bf16[64,4096]{1,0:T(8,128)(2,1)S(1)}, u32[]{:S(2)}, u32[]{:S(2)}) %collective-permute-start.6) | collective-permute-done | bytes 524320 | tf_op jit(solution)/shard_map/ppermute | solution.py:67
  489.2 12.2 %collective-permute-done.5 = bf16[64,4096]{1,0:T(8,128)(2,1)S(1)} collective-permute-done((bf16[64,4096]{1,0:T(8,128)(2,1)S(1)}, bf16[64,4096]{1,0:T(8,128)(2,1)S(1)}, u32[]{:S(2)}, u32[]{:S(2)}) %collective-permute-start.5) | collective-permute-done | bytes 524320 | tf_op jit(solution)/shard_map/ppermute | solution.py:65
  501.5 16.0 %fusion.36 = f32[4096,2048]{1,0:T(8,128)} fusion(bf16[256,2048]{1,0:T(8,128)(2,1)S(1)} %broadcast_select_fusion, s32[]{:T(128)S(6)} %select_n.28, bf16[64,4096]{1,0:T(8,128)(2,1)S(1)} %collective-permute-done.5, bf16[64,4096]{1,0:T(8,128)(2,1)S(1)} %collective-permute-done.4, bf16[64,4096]{1,0:T(8,128)(2,1)S(1)} %get-tuple-element.31, ...), kind=kOutput, calls=%fused_computation.42 | convolution fusion | flops 4311744512 | bytes 36700164 | tf_op jit(solution)/shard_map/dot_general | solution.py:71
  517.5 12.0 %fusion.29 = bf16[256,2048]{1,0:T(8,128)(2,1)} fusion(bf16[256,4096]{1,0:T(8,128)(2,1)} %all-gather.19.cloned.1.call-done, bf16[1,2048,4096]{2,1,0:T(8,128)(2,1)} %param.14), kind=kOutput, calls=%fused_computation.37 | convolution fusion | flops 4295491584 | bytes 19922944 | tf_op jit(solution)/shard_map/dot_general | solution.py:88
  529.5 22.3 %fusion.1 = bf16[1,4096,2048]{2,1,0:T(8,128)(2,1)} fusion(f32[4096,2048]{1,0:T(8,128)} %fusion.36, s32[]{:T(128)S(6)} %select_n.28, bf16[64,4096]{1,0:T(8,128)(2,1)} %collective-permute-done.2, bf16[64,4096]{1,0:T(8,128)(2,1)} %collective-permute-done.1, bf16[64,4096]{1,0:T(8,128)(2,1)S(1)} %get-tuple-element.29, ...), kind=kOutput, calls=%fused_computation.3 | convolution fusion | flops 4336910336 | bytes 53477380 | tf_op jit(solution)/shard_map/dot_general | solution.py:71
  551.8 19.6 %fusion = bf16[1,2048,4096]{2,1,0:T(8,128)(2,1)} fusion(f32[2048,4096]{1,0:T(8,128)} %fusion.110, bf16[256,2048]{1,0:T(8,128)(2,1)} %all-gather.17.cloned.1.call-done, bf16[256,4096]{1,0:T(8,128)(2,1)} %all-gather.19.cloned.1.call-done), kind=kOutput, calls=%fused_computation.2 | convolution fusion | flops 4320133120 | bytes 53477376 | tf_op jit(solution)/shard_map/dot_general | solution.py:85
  572.8 8.4 %all-reduce.1 = (f32[64,1]{0,1:T(1,128)S(1)}, f32[64,1]{0,1:T(1,128)S(1)}) all-reduce(f32[64,1]{0,1:T(1,128)S(1)} %bitcast.166, f32[64,1]{0,1:T(1,128)S(1)} %bitcast.167), channel_id=1, replica_groups=mesh['section'=2,'dp'=4,'tensor'=4] {'dp'}, use_global_device_ids=true, to_apply=%region_21.22 | all-reduce | flops 128 | bytes 1024 | tf_op jit(solution)/shard_map/psum | solution.py:98
  581.2 10.1 %all-reduce = (f32[2048]{0:T(1024)S(1)}, f32[2048]{0:T(1024)S(1)}) all-reduce(f32[2048]{0:T(1024)S(1)} %add.114, f32[2048]{0:T(1024)S(1)} %add.115), channel_id=1, replica_groups=mesh['section'=2,'dp'=4,'tensor'=4] {'tensor'}, use_global_device_ids=true, to_apply=%region_24.26 | all-reduce | flops 4096 | bytes 32768 | tf_op jit(solution)/shard_map/psum | solution.py:139
  (65 shorter events, 24.0 us)
Async XLA Ops:
  7.2 32.8 %all-gather.9.cloned.1.call-start = ((), (), s32[]{:S(2)}) async-start(), calls=%async_computation.7 | async-start | bytes 1310720 | tf_op jit(solution)/shard_map/all_gather | solution.py:49
  24.9 33.4 %all-gather.21.cloned.1.call-start = ((), (), s32[]{:S(2)}) async-start(), calls=%async_computation.18 | async-start | bytes 1310720 | tf_op jit(solution)/shard_map/all_gather | solution.py:123
  25.6 79.4 %reduce-scatter.9.cloned.1.call-start = ((), (), s32[]{:S(2)}) async-start(), calls=%async_computation.8 | async-start | bytes 2621440 | tf_op jit(solution)/shard_map/reduce_scatter | solution.py:51
  51.9 99.2 %reduce-scatter.7.cloned.1.call-start = ((), (), s32[]{:S(2)}) async-start(), calls=%async_computation.6 | async-start | bytes 2621440 | tf_op jit(solution)/shard_map/reduce_scatter | solution.py:73
  70.3 128.9 %all-gather.11.cloned.1.call-start = ((), (), s32[]{:S(2)}) async-start(), calls=%async_computation.9 | async-start | bytes 2621440 | tf_op jit(solution)/shard_map/all_gather | solution.py:84
  153.7 81.1 %copy-start = (bf16[1,2,64,2048]{3,2,1,0:T(8,128)(2,1)S(1)}, bf16[1,2,64,2048]{3,2,1,0:T(8,128)(2,1)}, u32[]{:S(2)}) copy-start(bf16[1,2,64,2048]{3,2,1,0:T(8,128)(2,1)} %param.9) | copy-start | bytes 1572868
  153.7 81.1 %copy-start.3 = (f32[1,2048]{1,0:T(1,128)S(1)}, f32[1,2048]{1,0:T(1,128)}, u32[]{:S(2)}) copy-start(f32[1,2048]{1,0:T(1,128)} %param.12) | copy-start | bytes 24580
  153.8 94.2 %copy-start.4 = (f32[1,2048]{1,0:T(1,128)S(1)}, f32[1,2048]{1,0:T(1,128)}, u32[]{:S(2)}) copy-start(f32[1,2048]{1,0:T(1,128)} %param.13) | copy-start | bytes 24580
  153.8 81.1 %reduce-scatter.11.cloned.1.call-start = ((), (), s32[]{:S(2)}) async-start(), calls=%async_computation.10 | async-start | bytes 1310720 | tf_op jit(solution)/shard_map/reduce_scatter | solution.py:87
  211.1 53.2 %all-gather.17.cloned.1.call-start = ((), (), s32[]{:S(2)}) async-start(), calls=%async_computation.14 | async-start | bytes 1310720 | tf_op jit(solution)/shard_map/all_gather | solution.py:49
  250.1 32.5 %all-gather.13.cloned.1.call-start = ((), (), s32[]{:S(2)}) async-start(), calls=%async_computation.11 | async-start | bytes 1310720 | tf_op jit(solution)/shard_map/all_gather | solution.py:130
  250.9 50.2 %all-gather.15.cloned.1.call-start = ((), (), s32[]{:S(2)}) async-start(), calls=%async_computation.12 | async-start | bytes 1310720 | tf_op jit(solution)/shard_map/all_gather | solution.py:124
  251.6 107.2 %reduce-scatter.15.cloned.1.call-start = ((), (), s32[]{:S(2)}) async-start(), calls=%async_computation.15 | async-start | bytes 2621440 | tf_op jit(solution)/shard_map/reduce_scatter | solution.py:51
  276.2 128.8 %reduce-scatter.13.cloned.1.call-start = ((), (), s32[]{:S(2)}) async-start(), calls=%async_computation.13 | async-start | bytes 2621440 | tf_op jit(solution)/shard_map/reduce_scatter | solution.py:73
  282.6 27.4 %collective-permute-start = (bf16[256,2048]{1,0:T(8,128)(2,1)}, bf16[256,2048]{1,0:T(8,128)(2,1)S(1)}, u32[]{:S(2)}, u32[]{:S(2)}) collective-permute-start(bf16[256,2048]{1,0:T(8,128)(2,1)} %all-gather.13.cloned.1.call-done), channel_id=1, source_target_pairs={{16,0},{17,1},{18,2},{19,3},{20,4},{21,5},{22,6},{23,7},{24,8},{25... | collective-permute-start | bytes 3145736 | tf_op jit(solution)/shard_map/ppermute | solution.py:16
  328.2 189.2 %all-gather.19.cloned.1.call-start = ((), (), s32[]{:S(2)}) async-start(), calls=%async_computation.16 | async-start | bytes 2621440 | tf_op jit(solution)/shard_map/all_gather | solution.py:84
  328.3 83.2 %collective-permute-start.1 = (bf16[64,4096]{1,0:T(8,128)(2,1)S(1)}, bf16[64,4096]{1,0:T(8,128)(2,1)}, u32[]{:S(2)}, u32[]{:S(2)}) collective-permute-start(bf16[64,4096]{1,0:T(8,128)(2,1)S(1)} %get-tuple-element.29), channel_id=1, source_target_pairs={{0,4},{4,8},{8,12},{12,0},{1,5},{5,9},{9,13},{13,1},{2,6},{6,10},{... | collective-permute-start | bytes 1572872 | tf_op jit(solution)/shard_map/ppermute | solution.py:65
  407.5 19.4 %collective-permute-start.4 = (bf16[64,4096]{1,0:T(8,128)(2,1)S(1)}, bf16[64,4096]{1,0:T(8,128)(2,1)S(1)}, u32[]{:S(2)}, u32[]{:S(2)}) collective-permute-start(bf16[64,4096]{1,0:T(8,128)(2,1)S(1)} %get-tuple-element.31), channel_id=1, source_target_pairs={{0,4},{4,8},{8,12},{12,0},{1,5},{5,9},{9,13},{13,1},{2,6},{6,10},{... | collective-permute-start | bytes 1572872 | tf_op jit(solution)/shard_map/ppermute | solution.py:65
  407.6 163.9 %reduce-scatter.17.cloned.1.call-start = ((), (), s32[]{:S(2)}) async-start(), calls=%async_computation.17 | async-start | bytes 1310720 | tf_op jit(solution)/shard_map/reduce_scatter | solution.py:87
  407.6 121.9 %collective-permute-start.3 = (bf16[64,4096]{1,0:T(8,128)(2,1)S(1)}, bf16[64,4096]{1,0:T(8,128)(2,1)}, u32[]{:S(2)}, u32[]{:S(2)}) collective-permute-start(bf16[64,4096]{1,0:T(8,128)(2,1)S(1)} %get-tuple-element.29), channel_id=1, source_target_pairs={{0,12},{4,0},{8,4},{12,8},{1,13},{5,1},{9,5},{13,9},{2,14},{6,2},{... | collective-permute-start | bytes 1572872 | tf_op jit(solution)/shard_map/ppermute | solution.py:67
  411.5 118.0 %collective-permute-start.2 = (bf16[64,4096]{1,0:T(8,128)(2,1)}, bf16[64,4096]{1,0:T(8,128)(2,1)}, u32[]{:S(2)}, u32[]{:S(2)}) collective-permute-start(bf16[64,4096]{1,0:T(8,128)(2,1)} %collective-permute-done.1), channel_id=1, source_target_pairs={{0,4},{4,8},{8,12},{12,0},{1,5},{5,9},{9,13},{13,1},{2,6},{6,10},{... | collective-permute-start | bytes 1572872 | tf_op jit(solution)/shard_map/ppermute | solution.py:65
  411.5 77.7 %collective-permute-start.6 = (bf16[64,4096]{1,0:T(8,128)(2,1)S(1)}, bf16[64,4096]{1,0:T(8,128)(2,1)S(1)}, u32[]{:S(2)}, u32[]{:S(2)}) collective-permute-start(bf16[64,4096]{1,0:T(8,128)(2,1)S(1)} %get-tuple-element.31), channel_id=1, source_target_pairs={{0,12},{4,0},{8,4},{12,8},{1,13},{5,1},{9,5},{13,9},{2,14},{6,2},{... | collective-permute-start | bytes 1572872 | tf_op jit(solution)/shard_map/ppermute | solution.py:67
  426.9 74.5 %collective-permute-start.5 = (bf16[64,4096]{1,0:T(8,128)(2,1)S(1)}, bf16[64,4096]{1,0:T(8,128)(2,1)S(1)}, u32[]{:S(2)}, u32[]{:S(2)}) collective-permute-start(bf16[64,4096]{1,0:T(8,128)(2,1)S(1)} %collective-permute-done.4), channel_id=1, source_target_pairs={{0,4},{4,8},{8,12},{12,0},{1,5},{5,9},{9,13},{13,1},{2,6},{6,10},{... | collective-permute-start | bytes 1572872 | tf_op jit(solution)/shard_map/ppermute | solution.py:65
  517.5 12.1 %copy-start.2 = (bf16[1,256,2048]{2,1,0:T(8,128)(2,1)S(1)}, bf16[1,256,2048]{2,1,0:T(8,128)(2,1)}, u32[]{:S(2)}) copy-start(bf16[1,256,2048]{2,1,0:T(8,128)(2,1)} %all-gather.21.cloned.1.call-done) | copy-start | bytes 3145732
  551.8 42.0 %copy-start.1 = (bf16[64,2048]{1,0:T(8,128)(2,1)S(1)}, bf16[64,2048]{1,0:T(8,128)(2,1)}, u32[]{:S(2)}) copy-start(bf16[64,2048]{1,0:T(8,128)(2,1)} %get-tuple-element.27) | copy-start | bytes 786436
Sparse Core Ops, SparseCore 0:
  25.0 14.9 all-gather.8
  41.5 16.7 all-gather.20
  61.2 43.8 reduce-scatter.8
  107.9 43.1 reduce-scatter.6
  153.9 45.2 all-gather.10
  211.2 23.5 reduce-scatter.10
  250.2 13.9 all-gather.16
  265.9 16.7 all-gather.12
  284.3 16.7 all-gather.14
  303.8 54.9 reduce-scatter.14
  361.7 43.1 reduce-scatter.12
  407.7 77.3 all-gather.18
  529.6 23.0 reduce-scatter.16
